TPU v7x, 32 devices: a whole 2x2x4 slice. The times are simulated.
32 devices in a mesh: ctx: 16 (over z, y, x), head: 2 (over core).
Axes of the slice: x: 2, y: 2, z: 4, core: 2. Of those that a mesh axis runs over, the one named last changes fastest.
Arguments:
- q_nope: bfloat16 [1024, 16, 128], P('ctx', 'head'), may hold values from -6 to 6
- q_rope: bfloat16 [1024, 16, 64], P('ctx', 'head'), may hold values from -8 to 8
- latent_cache: bfloat16 [1024, 576], P(('ctx', 'head')), may hold values from -8 to 8
- positions: int32 [1024], P(('ctx', 'head')), may hold values from 0 to 1023, as said below
- w_uk: bfloat16 [16, 128, 512], P('head'), may hold values from -0.5 to 0.5
- w_uv: bfloat16 [16, 512, 128], P('head'), may hold values from -0.25 to 0.25
Outputs:
- attended: bfloat16 [1024, 2048], P('ctx', 'head')
Inputs may be any that keep to these rules, and one draw needn't show every extreme that they name: positions holds each of 0 to 1023 once; each aligned block of 64 entries holds consecutive positions in increasing order, starting at a multiple of 64; the blocks' order is arbitrary.
All inputs are finite; a program needn't handle non-finite values.
Results may differ from a plain program's by a relative error of at most 0.0065.
Values may be sent and summed in bfloat16 or wider, within the bound.
A program may use at most 64 MiB of HBM per device.

v0:
```python
import jax
import jax.numpy as jnp
from jax import lax
from jax.sharding import PartitionSpec as P


def shards(q_nope, q_rope, latent_cache, positions, w_uk, w_uv):
    token_count, head_count, nope_width = q_nope.shape
    latent_width = w_uk.shape[2]
    seq_length = token_count * lax.axis_size("ctx")
    scale_factor = float(nope_width + q_rope.shape[2]) ** (-0.5)
    query_latent = jnp.einsum(
        "thn,hnc->thc", q_nope, w_uk, preferred_element_type=jnp.float32
    ).astype(jnp.bfloat16)
    query_full = jnp.concatenate([query_latent, q_rope], axis=2).reshape(
        token_count * head_count, -1
    )
    query_rows = token_count * head_count
    query_pos = lax.all_gather(positions, "head", axis=0, tiled=True)
    row_pos = jnp.repeat(query_pos, head_count)
    first_query = jnp.min(query_pos)
    seq_start = first_query - first_query % seq_length
    upper_bound = seq_start + seq_length - 1

    def attend(state_now, key_block):
        cache_block, key_pos = key_block
        run_max, run_sum, run_acc = state_now
        scores = (
            lax.dot_general(
                query_full,
                cache_block,
                (((1,), (1,)), ((), ())),
                preferred_element_type=jnp.float32,
            )
            * scale_factor
        )
        allowed = (row_pos[:, None] >= key_pos[None, :]) & (key_pos[None, :] >= seq_start)
        scores = jnp.where(allowed, scores, -jnp.inf)
        new_max = jnp.maximum(run_max, jnp.max(scores, axis=1))
        rescale = jnp.exp(run_max - new_max)
        expo = jnp.exp(scores - new_max[:, None])
        new_sum = run_sum * rescale + jnp.sum(expo, axis=1)
        new_acc = run_acc * rescale[:, None] + jnp.dot(
            expo.astype(jnp.bfloat16),
            cache_block[:, :latent_width],
            preferred_element_type=jnp.float32,
        )
        return (new_max, new_sum, new_acc)

    def unchanged(state_now, key_block):
        return state_now

    def visit_block(state_now, key_block):
        key_pos = key_block[1]
        wanted = jnp.any((key_pos >= seq_start) & (key_pos <= upper_bound))
        return lax.cond(wanted, attend, unchanged, state_now, key_block)

    start_state = (
        jnp.full((query_rows,), -1e30, jnp.float32),
        jnp.zeros((query_rows,), jnp.float32),
        jnp.zeros((query_rows, latent_width), jnp.float32),
    )
    cache_piece = lax.all_gather(latent_cache, ("ctx", "head"), axis=0, tiled=True)
    pos_piece = lax.all_gather(positions, ("ctx", "head"), axis=0, tiled=True)
    row_total = cache_piece.shape[0]
    key_blocks = (
        cache_piece.reshape(row_total // token_count, token_count, cache_piece.shape[1]),
        pos_piece.reshape(row_total // token_count, token_count),
    )

    def advance(inner_state, key_block):
        return (visit_block(inner_state, key_block), None)

    final_state, unused = lax.scan(advance, start_state, key_blocks)
    run_max, run_sum, run_acc = final_state
    latent_out = (
        (run_acc / run_sum[:, None])
        .astype(jnp.bfloat16)
        .reshape(token_count, head_count, latent_width)
    )
    attended = jnp.einsum(
        "thc,hcv->thv", latent_out, w_uv, preferred_element_type=jnp.float32
    ).astype(jnp.bfloat16)
    return attended.reshape(token_count, head_count * attended.shape[2])


def solution(mesh):
    placed = (
        P("ctx", "head", None),
        P("ctx", "head", None),
        P(("ctx", "head"), None),
        P(("ctx", "head")),
        P("head", None, None),
        P("head", None, None),
    )
    return jax.shard_map(
        shards, mesh=mesh, in_specs=placed, out_specs=P("ctx", "head"), check_vma=False
    )
```

profile of v0, /device:TPU:0, one launch (start us, length us, event | category | flops | bytes accessed | tf_op | source)
XLA Modules:
  0.0 129.4 jit_solution(7734954087094462420)
XLA Ops:
  7.3 1.3 dynamic-slice
  10.0 1.9 %all-reduce.1 = s32[64]{0:T(128)S(1)} all-reduce(s32[64]{0:T(128)S(1)} %dynamic-update-slice.1), channel_id=1, replica_groups=mesh['ctx'=16,'head'=2] {'head'}, use_global_device_ids=true, to_apply=%add.1 | all-reduce | flops 64 | bytes 512
  15.8 41.9 %all-reduce = s32[1024]{0:T(1024)S(1)} all-reduce(s32[1024]{0:T(1024)S(1)} %dynamic-update-slice), channel_id=1, replica_groups=mesh['ctx'=16,'head'=2] {'ctx','head'}, use_global_device_ids=true, to_apply=%add | all-reduce | flops 1024 | bytes 8192
  57.7 0.9 copy.11
  58.7 1.2 fusion.9
  60.4 6.8 %all-gather.2.cloned.1.call-done = bf16[1024,576]{1,0:T(8,128)(2,1)} async-done(((bf16[32,576]{1,0:T(8,128)(2,1)}), bf16[1024,576]{1,0:T(8,128)(2,1)}) %all-gather.2.cloned.1.call-update) | async-done | bytes 1179664 | tf_op jit(solution)/shard_map/all_gather | solution.py:63
  67.4 52.9 %while.15 = (s32[]{:T(128)}, f32[512]{0:T(512)S(1)}, f32[512]{0:T(512)S(1)}, f32[512,512]{1,0:T(8,128)S(1)}, s32[16,64]{1,0:T(8,128)S(1)}, /*index=5*/s32[]{:T(1...) while((s32[]{:T(128)}, f32[512]{0:T(512)S(1)}, ...), condition=%wide.region_7.8_spmd.clone, body=%wide.region_1.7_spmd.clone.sunk | while | flops 72123712 | bytes 3409543 | solution.py:74
  68.7 2.0 %conditional.3 = ((f32[512]{0:T(512)S(1)}, f32[512]{0:T(512)S(1)}, f32[512,512]{1,0:T(8,128)S(1)})) conditional(s32[]{:T(128)} %convert_element_type.40, (f32[512]{0:T(512)S(1)}, f32[512]{0:T(512)S(1)}, f32[512,512]{1,0:T(8,128)S(1)}) %tuple.39, (s32[64]{0:T(128)S(1)}, s32[64]{0:T(128)S(1)}, s32[]{:T(128)}, bf16[16,64,576]{2,1,0:T(8,128)(2,1)}, ...), branch_computations={%region_3.3_spmd, %region_4.6_spmd} | conditional | flops 72123456 | bytes 3408808 | solution.py:56
  72.0 2.0 %conditional.3 = ((f32[512]{0:T(512)S(1)}, f32[512]{0:T(512)S(1)}, f32[512,512]{1,0:T(8,128)S(1)})) conditional(s32[]{:T(128)} %convert_element_type.40, (f32[512]{0:T(512)S(1)}, f32[512]{0:T(512)S(1)}, f32[512,512]{1,0:T(8,128)S(1)}) %tuple.39, (s32[64]{0:T(128)S(1)}, s32[64]{0:T(128)S(1)}, s32[]{:T(128)}, bf16[16,64,576]{2,1,0:T(8,128)(2,1)}, ...), branch_computations={%region_3.3_spmd, %region_4.6_spmd} | conditional | flops 72123456 | bytes 3408808 | solution.py:56
  75.3 2.0 %conditional.3 = ((f32[512]{0:T(512)S(1)}, f32[512]{0:T(512)S(1)}, f32[512,512]{1,0:T(8,128)S(1)})) conditional(s32[]{:T(128)} %convert_element_type.40, (f32[512]{0:T(512)S(1)}, f32[512]{0:T(512)S(1)}, f32[512,512]{1,0:T(8,128)S(1)}) %tuple.39, (s32[64]{0:T(128)S(1)}, s32[64]{0:T(128)S(1)}, s32[]{:T(128)}, bf16[16,64,576]{2,1,0:T(8,128)(2,1)}, ...), branch_computations={%region_3.3_spmd, %region_4.6_spmd} | conditional | flops 72123456 | bytes 3408808 | solution.py:56
  75.3 0.9 dynamic-slice_bitcast_fusion
  78.6 2.0 %conditional.3 = ((f32[512]{0:T(512)S(1)}, f32[512]{0:T(512)S(1)}, f32[512,512]{1,0:T(8,128)S(1)})) conditional(s32[]{:T(128)} %convert_element_type.40, (f32[512]{0:T(512)S(1)}, f32[512]{0:T(512)S(1)}, f32[512,512]{1,0:T(8,128)S(1)}) %tuple.39, (s32[64]{0:T(128)S(1)}, s32[64]{0:T(128)S(1)}, s32[]{:T(128)}, bf16[16,64,576]{2,1,0:T(8,128)(2,1)}, ...), branch_computations={%region_3.3_spmd, %region_4.6_spmd} | conditional | flops 72123456 | bytes 3408808 | solution.py:56
  81.9 2.0 %conditional.3 = ((f32[512]{0:T(512)S(1)}, f32[512]{0:T(512)S(1)}, f32[512,512]{1,0:T(8,128)S(1)})) conditional(s32[]{:T(128)} %convert_element_type.40, (f32[512]{0:T(512)S(1)}, f32[512]{0:T(512)S(1)}, f32[512,512]{1,0:T(8,128)S(1)}) %tuple.39, (s32[64]{0:T(128)S(1)}, s32[64]{0:T(128)S(1)}, s32[]{:T(128)}, bf16[16,64,576]{2,1,0:T(8,128)(2,1)}, ...), branch_computations={%region_3.3_spmd, %region_4.6_spmd} | conditional | flops 72123456 | bytes 3408808 | solution.py:56
  85.2 2.0 %conditional.3 = ((f32[512]{0:T(512)S(1)}, f32[512]{0:T(512)S(1)}, f32[512,512]{1,0:T(8,128)S(1)})) conditional(s32[]{:T(128)} %convert_element_type.40, (f32[512]{0:T(512)S(1)}, f32[512]{0:T(512)S(1)}, f32[512,512]{1,0:T(8,128)S(1)}) %tuple.39, (s32[64]{0:T(128)S(1)}, s32[64]{0:T(128)S(1)}, s32[]{:T(128)}, bf16[16,64,576]{2,1,0:T(8,128)(2,1)}, ...), branch_computations={%region_3.3_spmd, %region_4.6_spmd} | conditional | flops 72123456 | bytes 3408808 | solution.py:56
  88.5 2.0 %conditional.3 = ((f32[512]{0:T(512)S(1)}, f32[512]{0:T(512)S(1)}, f32[512,512]{1,0:T(8,128)S(1)})) conditional(s32[]{:T(128)} %convert_element_type.40, (f32[512]{0:T(512)S(1)}, f32[512]{0:T(512)S(1)}, f32[512,512]{1,0:T(8,128)S(1)}) %tuple.39, (s32[64]{0:T(128)S(1)}, s32[64]{0:T(128)S(1)}, s32[]{:T(128)}, bf16[16,64,576]{2,1,0:T(8,128)(2,1)}, ...), branch_computations={%region_3.3_spmd, %region_4.6_spmd} | conditional | flops 72123456 | bytes 3408808 | solution.py:56
  91.8 2.0 %conditional.3 = ((f32[512]{0:T(512)S(1)}, f32[512]{0:T(512)S(1)}, f32[512,512]{1,0:T(8,128)S(1)})) conditional(s32[]{:T(128)} %convert_element_type.40, (f32[512]{0:T(512)S(1)}, f32[512]{0:T(512)S(1)}, f32[512,512]{1,0:T(8,128)S(1)}) %tuple.39, (s32[64]{0:T(128)S(1)}, s32[64]{0:T(128)S(1)}, s32[]{:T(128)}, bf16[16,64,576]{2,1,0:T(8,128)(2,1)}, ...), branch_computations={%region_3.3_spmd, %region_4.6_spmd} | conditional | flops 72123456 | bytes 3408808 | solution.py:56
  91.8 0.9 dynamic-slice_bitcast_fusion
  95.1 2.0 %conditional.3 = ((f32[512]{0:T(512)S(1)}, f32[512]{0:T(512)S(1)}, f32[512,512]{1,0:T(8,128)S(1)})) conditional(s32[]{:T(128)} %convert_element_type.40, (f32[512]{0:T(512)S(1)}, f32[512]{0:T(512)S(1)}, f32[512,512]{1,0:T(8,128)S(1)}) %tuple.39, (s32[64]{0:T(128)S(1)}, s32[64]{0:T(128)S(1)}, s32[]{:T(128)}, bf16[16,64,576]{2,1,0:T(8,128)(2,1)}, ...), branch_computations={%region_3.3_spmd, %region_4.6_spmd} | conditional | flops 72123456 | bytes 3408808 | solution.py:56
  95.1 0.9 dynamic-slice_bitcast_fusion
  98.4 2.0 %conditional.3 = ((f32[512]{0:T(512)S(1)}, f32[512]{0:T(512)S(1)}, f32[512,512]{1,0:T(8,128)S(1)})) conditional(s32[]{:T(128)} %convert_element_type.40, (f32[512]{0:T(512)S(1)}, f32[512]{0:T(512)S(1)}, f32[512,512]{1,0:T(8,128)S(1)}) %tuple.39, (s32[64]{0:T(128)S(1)}, s32[64]{0:T(128)S(1)}, s32[]{:T(128)}, bf16[16,64,576]{2,1,0:T(8,128)(2,1)}, ...), branch_computations={%region_3.3_spmd, %region_4.6_spmd} | conditional | flops 72123456 | bytes 3408808 | solution.py:56
  98.4 0.9 dynamic-slice_bitcast_fusion
  101.7 2.0 %conditional.3 = ((f32[512]{0:T(512)S(1)}, f32[512]{0:T(512)S(1)}, f32[512,512]{1,0:T(8,128)S(1)})) conditional(s32[]{:T(128)} %convert_element_type.40, (f32[512]{0:T(512)S(1)}, f32[512]{0:T(512)S(1)}, f32[512,512]{1,0:T(8,128)S(1)}) %tuple.39, (s32[64]{0:T(128)S(1)}, s32[64]{0:T(128)S(1)}, s32[]{:T(128)}, bf16[16,64,576]{2,1,0:T(8,128)(2,1)}, ...), branch_computations={%region_3.3_spmd, %region_4.6_spmd} | conditional | flops 72123456 | bytes 3408808 | solution.py:56
  101.7 0.9 dynamic-slice_bitcast_fusion
  105.0 2.0 %conditional.3 = ((f32[512]{0:T(512)S(1)}, f32[512]{0:T(512)S(1)}, f32[512,512]{1,0:T(8,128)S(1)})) conditional(s32[]{:T(128)} %convert_element_type.40, (f32[512]{0:T(512)S(1)}, f32[512]{0:T(512)S(1)}, f32[512,512]{1,0:T(8,128)S(1)}) %tuple.39, (s32[64]{0:T(128)S(1)}, s32[64]{0:T(128)S(1)}, s32[]{:T(128)}, bf16[16,64,576]{2,1,0:T(8,128)(2,1)}, ...), branch_computations={%region_3.3_spmd, %region_4.6_spmd} | conditional | flops 72123456 | bytes 3408808 | solution.py:56
  108.3 2.0 %conditional.3 = ((f32[512]{0:T(512)S(1)}, f32[512]{0:T(512)S(1)}, f32[512,512]{1,0:T(8,128)S(1)})) conditional(s32[]{:T(128)} %convert_element_type.40, (f32[512]{0:T(512)S(1)}, f32[512]{0:T(512)S(1)}, f32[512,512]{1,0:T(8,128)S(1)}) %tuple.39, (s32[64]{0:T(128)S(1)}, s32[64]{0:T(128)S(1)}, s32[]{:T(128)}, bf16[16,64,576]{2,1,0:T(8,128)(2,1)}, ...), branch_computations={%region_3.3_spmd, %region_4.6_spmd} | conditional | flops 72123456 | bytes 3408808 | solution.py:56
  108.3 0.9 dynamic-slice_bitcast_fusion
  111.6 2.0 %conditional.3 = ((f32[512]{0:T(512)S(1)}, f32[512]{0:T(512)S(1)}, f32[512,512]{1,0:T(8,128)S(1)})) conditional(s32[]{:T(128)} %convert_element_type.40, (f32[512]{0:T(512)S(1)}, f32[512]{0:T(512)S(1)}, f32[512,512]{1,0:T(8,128)S(1)}) %tuple.39, (s32[64]{0:T(128)S(1)}, s32[64]{0:T(128)S(1)}, s32[]{:T(128)}, bf16[16,64,576]{2,1,0:T(8,128)(2,1)}, ...), branch_computations={%region_3.3_spmd, %region_4.6_spmd} | conditional | flops 72123456 | bytes 3408808 | solution.py:56
  111.6 0.9 dynamic-slice_bitcast_fusion
  114.9 2.0 %conditional.3 = ((f32[512]{0:T(512)S(1)}, f32[512]{0:T(512)S(1)}, f32[512,512]{1,0:T(8,128)S(1)})) conditional(s32[]{:T(128)} %convert_element_type.40, (f32[512]{0:T(512)S(1)}, f32[512]{0:T(512)S(1)}, f32[512,512]{1,0:T(8,128)S(1)}) %tuple.39, (s32[64]{0:T(128)S(1)}, s32[64]{0:T(128)S(1)}, s32[]{:T(128)}, bf16[16,64,576]{2,1,0:T(8,128)(2,1)}, ...), branch_computations={%region_3.3_spmd, %region_4.6_spmd} | conditional | flops 72123456 | bytes 3408808 | solution.py:56
  115.0 0.9 dynamic-slice_bitcast_fusion
  118.2 2.0 %conditional.3 = ((f32[512]{0:T(512)S(1)}, f32[512]{0:T(512)S(1)}, f32[512,512]{1,0:T(8,128)S(1)})) conditional(s32[]{:T(128)} %convert_element_type.40, (f32[512]{0:T(512)S(1)}, f32[512]{0:T(512)S(1)}, f32[512,512]{1,0:T(8,128)S(1)}) %tuple.39, (s32[64]{0:T(128)S(1)}, s32[64]{0:T(128)S(1)}, s32[]{:T(128)}, bf16[16,64,576]{2,1,0:T(8,128)(2,1)}, ...), branch_computations={%region_3.3_spmd, %region_4.6_spmd} | conditional | flops 72123456 | bytes 3408808 | solution.py:56
  120.4 1.1 copy-done.1
  (187 shorter events, 39.4 us)
Async XLA Ops:
  6.5 52.1 %copy-start = (bf16[8,128,512]{2,1,0:T(8,128)(2,1)S(1)}, bf16[8,128,512]{2,1,0:T(8,128)(2,1)}, u32[]{:S(2)}) copy-start(bf16[8,128,512]{2,1,0:T(8,128)(2,1)} %param.14) | copy-start | bytes 3145732
  6.5 60.7 %all-gather.2.cloned.1.call-start = ((), (), s32[]{:S(2)}) async-start(), calls=%async_computation | async-start | bytes 1351680 | tf_op jit(solution)/shard_map/all_gather | solution.py:63
  120.3 1.2 copy-start.1
Sparse Core Ops, SparseCore 0:
  10.2 56.9 all-gather.1
where the time goes:
time: 130 us; the launch traced here: 129 us
  blocking collectives  43.8 us (34%)
  local copies, waits for them, and re-layouts  23.3 us (18%)
  between operations  16.4 us (13%)
  matrix products  14.6 us (11%)
  other arithmetic  12.5 us (10%)
  loops' own time  11.2 us (9%)
  waiting for transfers between devices  7.56 us (6%)
    unnamed x2, blocking collectives  43.8 us
    squeeze x16, local copies, waits for them, and re-layouts, shards(): final_state, unused = lax.scan(advance, start_state, key_blocks)  14.4 us
    reduce_or x16, other arithmetic, visit_block(): wanted = jnp.any((key_pos >= seq_start) & (key_pos <= upper_bound))  10.5 us
    another operation x1, loops' own time, shards(): final_state, unused = lax.scan(advance, start_state, key_blocks)  10.5 us
    dot_general x16, matrix products, attend(): jnp.dot(expo.astype(jnp.bfloat16), cache_block[:, :latent_width], preferr...  7.54 us
    all_gather x1, waiting for transfers between devices, shards(): lax.all_gather(latent_cache, ('ctx', 'head'), axis=0, tiled=True)  6.85 us
    dot_general x16, matrix products, attend(): lax.dot_general(query_full, cache_block, (((1,), (1,)), ((), ())), prefer...  5.42 us
    unnamed x10, local copies, waits for them, and re-layouts  5 us
  transfers between devices with their start and end apart: 1, of which 1 were waited for; matrix products, arithmetic and copies ran while one was open for 5% of the time, Pallas kernels for 0%

commit v1 on v0

--- a/solution.py
+++ b/solution.py
@@ -1,6 +1,10 @@
+import functools
+
 import jax
 import jax.numpy as jnp
 from jax import lax
+from jax.experimental import pallas as pl
+from jax.experimental.pallas import tpu as pltpu
 from jax.sharding import PartitionSpec as P
 
 
@@ -84,6 +88,210 @@
     return attended.reshape(token_count, head_count * attended.shape[2])
 
 
+MESH = pl.DeviceIdType.MESH
+
+
+def kernel(
+    seq_length, scale_factor,
+    nope_ref, rope_ref, pay_ref, uk_hbm, uv_hbm, out_ref,
+    keys, uk, uv, nope_f, rope_f, query, scores, probs,
+    local_sem, send_sem, recv_sem,
+):
+    tokens, heads, _ = nope_ref.shape
+    latent = uk.shape[2]
+    value_width = uv.shape[2]
+    shard, width = pay_ref.shape
+    ctx, core = lax.axis_index("ctx"), lax.axis_index("head")
+    z, y, x = ctx // 4, (ctx // 2) % 2, ctx % 2
+    copy_uk = pltpu.make_async_copy(uk_hbm, uk, local_sem.at[0])
+    copy_uv = pltpu.make_async_copy(uv_hbm, uv, local_sem.at[1])
+    copy_uk.start()
+    copy_uv.start()
+
+    def index_of(zi, yi, xi):
+        return (zi * 2 + yi) * 2 + xi
+
+    def line_of(c, yi, xi):
+        return (c * 2 + yi) * 2 + xi
+
+    def slot_of(line, zi):
+        return line * 4 + zi
+
+    x2 = x + (1 - core) * (1 - 2 * x)
+    y2 = y + core * (1 - 2 * y)
+    x3 = x + core * (1 - 2 * x)
+    y3 = y + (1 - core) * (1 - 2 * y)
+    second = (index_of(z, y2, x2), core)
+    third = (index_of(z, y3, x3), core)
+    partner = (ctx, 1 - core)
+    along = [(index_of((z + k) % 4, y, x), core) for k in (1, 2, 3)]
+
+    barrier = pltpu.get_barrier_semaphore()
+    for peer in along + [second, third, partner]:
+        pl.semaphore_signal(barrier, inc=1, device_id=peer, device_id_type=MESH)
+
+    line_own = line_of(core, y, x)
+    line_second = line_of(core, y2, x2)
+    line_third = line_of(core, y3, x3)
+    line_both = line_of(core, 1 - y, 1 - x)
+    own = slot_of(line_own, z)
+
+    def rows_of(slot):
+        return keys.at[pl.ds(pl.multiple_of(slot * shard, shard), shard)]
+
+    keys[pl.ds(pl.multiple_of(own * shard, shard), shard), :] = pay_ref[...]
+    pl.semaphore_wait(barrier, 6)
+
+    sends = []
+
+    def send(slot, peer):
+        copy = pltpu.make_async_remote_copy(
+            src_ref=rows_of(slot), dst_ref=rows_of(slot),
+            send_sem=send_sem.at[len(sends)], recv_sem=recv_sem.at[slot],
+            device_id=peer, device_id_type=MESH,
+        )
+        copy.start()
+        sends.append(copy)
+
+    def arrived(slot):
+        pltpu.make_async_remote_copy(
+            src_ref=rows_of(slot), dst_ref=rows_of(slot),
+            send_sem=send_sem.at[0], recv_sem=recv_sem.at[slot],
+            device_id=partner, device_id_type=MESH,
+        ).wait_recv()
+
+    def score(line):
+        columns = pl.ds(pl.multiple_of(line * 128, 128), 128)
+        scores[:, columns] = lax.dot_general(
+            query[...], keys[columns, :], (((1,), (1,)), ((), ())),
+            preferred_element_type=jnp.float32,
+        )
+
+    for peer in along:
+        send(own, peer)
+    send(own, second)
+    send(own, third)
+    send(own, partner)
+
+    nope_f[...] = nope_ref[...].astype(jnp.float32)
+    rope_f[...] = rope_ref[...].astype(jnp.float32)
+    copy_uk.wait()
+    for h in range(heads):
+        rows = pl.ds(h * tokens, tokens)
+        query[rows, :latent] = jnp.dot(
+            nope_f[:, h, :].astype(jnp.bfloat16), uk[h],
+            preferred_element_type=jnp.float32,
+        ).astype(jnp.bfloat16)
+        rope_h = rope_f[:, h, :]
+        query[rows, latent:] = jnp.concatenate(
+            [rope_h, jnp.zeros((tokens, width - latent - rope_h.shape[1]), jnp.float32)],
+            axis=1,
+        ).astype(jnp.bfloat16)
+
+    for k in (1, 2, 3):
+        slot = slot_of(line_own, (z + 4 - k) % 4)
+        arrived(slot)
+        send(slot, second)
+        send(slot, third)
+        send(slot, partner)
+    for k in (0, 1, 2, 3):
+        slot = slot_of(line_second, (z + 4 - k) % 4)
+        arrived(slot)
+        send(slot, third)
+        send(slot, partner)
+    score(line_own)
+    score(line_second)
+    for line in (line_third, line_both):
+        for k in (0, 1, 2, 3):
+            slot = slot_of(line, (z + 4 - k) % 4)
+            arrived(slot)
+            send(slot, partner)
+        score(line)
+    other = 1 - core
+    for yi, xi in ((y, x), (y3, x3), (y2, x2), (1 - y, 1 - x)):
+        line = line_of(other, yi, xi)
+        for k in (0, 1, 2, 3):
+            arrived(slot_of(line, (z + 4 - k) % 4))
+        score(line)
+
+    lane = lax.broadcasted_iota(jnp.int32, (8, width - latent), 1)
+    first = rope_ref.shape[2]
+    pick = jnp.where(lane == first, 64.0, jnp.where(lane == first + 1, 1.0, 0.0))
+    key_pos = lax.dot_general(
+        pick.astype(jnp.bfloat16), keys[:, latent:], (((1,), (1,)), ((), ())),
+        preferred_element_type=jnp.float32,
+    )[0:1, :]
+    token_slots = [slot_of(line_of(c, y, x), z) for c in (0, 1)]
+    tails = jnp.concatenate(
+        [
+            keys[pl.ds(pl.multiple_of(s * shard, shard), shard), latent:]
+            for s in token_slots
+        ],
+        axis=0,
+    ).astype(jnp.float32)
+    query_pos = jnp.sum(tails * pick[0:1, :], axis=1, keepdims=True)
+    seq_start = jnp.floor(query_pos * (1.0 / seq_length)) * float(seq_length)
+    hidden = (key_pos > query_pos) | (key_pos < seq_start)
+    factor = scale_factor * 1.4426950408889634
+    sums = []
+    for h in range(heads):
+        rows = pl.ds(h * tokens, tokens)
+        s = jnp.where(hidden, -jnp.inf, scores[rows, :])
+        expo = jnp.exp2((s - jnp.max(s, axis=1, keepdims=True)) * factor)
+        sums.append(jnp.sum(expo, axis=1, keepdims=True))
+        probs[rows, :] = expo.astype(jnp.bfloat16)
+    mixed = jnp.dot(probs[...], keys[:, :latent], preferred_element_type=jnp.float32)
+    copy_uv.wait()
+    for h in range(heads):
+        part = (mixed[h * tokens : (h + 1) * tokens, :] / sums[h]).astype(jnp.bfloat16)
+        out_ref[:, h * value_width : (h + 1) * value_width] = jnp.dot(
+            part, uv[h], preferred_element_type=jnp.float32
+        ).astype(jnp.bfloat16)
+    for copy in sends:
+        copy.wait_send()
+
+
+def fused(q_nope, q_rope, latent_cache, positions, w_uk, w_uv):
+    tokens, heads, nope_width = q_nope.shape
+    latent = w_uk.shape[2]
+    shard, packed = latent_cache.shape
+    width = -(-(packed + 2) // 128) * 128
+    total = shard * lax.axis_size("ctx") * lax.axis_size("head")
+    place = jnp.stack([positions // 64, positions % 64], axis=1).astype(jnp.bfloat16)
+    payload = jnp.concatenate(
+        [latent_cache, place, jnp.zeros((shard, width - packed - 2), jnp.bfloat16)], axis=1
+    )
+    rows = tokens * heads
+    vmem = pl.BlockSpec(memory_space=pltpu.VMEM)
+    hbm = pl.BlockSpec(memory_space=pl.ANY)
+    flops = 2 * rows * (total * (width + latent) + latent * 2 * nope_width)
+    return pl.pallas_call(
+        functools.partial(kernel, total, float(nope_width + q_rope.shape[2]) ** (-0.5)),
+        out_shape=jax.ShapeDtypeStruct((tokens, heads * w_uv.shape[2]), jnp.bfloat16),
+        in_specs=[vmem, vmem, vmem, hbm, hbm],
+        out_specs=vmem,
+        scratch_shapes=[
+            pltpu.VMEM((total, width), jnp.bfloat16),
+            pltpu.VMEM(w_uk.shape, jnp.bfloat16),
+            pltpu.VMEM(w_uv.shape, jnp.bfloat16),
+            pltpu.VMEM(q_nope.shape, jnp.float32),
+            pltpu.VMEM(q_rope.shape, jnp.float32),
+            pltpu.VMEM((rows, width), jnp.bfloat16),
+            pltpu.VMEM((rows, total), jnp.float32),
+            pltpu.VMEM((rows, total), jnp.bfloat16),
+            pltpu.SemaphoreType.DMA((2,)),
+            pltpu.SemaphoreType.DMA((31,)),
+            pltpu.SemaphoreType.DMA((32,)),
+        ],
+        compiler_params=pltpu.CompilerParams(
+            collective_id=0, has_side_effects=True, vmem_limit_bytes=40 * 1024 * 1024
+        ),
+        cost_estimate=pl.CostEstimate(
+            flops=flops, bytes_accessed=4 * 1024 * 1024, transcendentals=rows * total
+        ),
+    )(q_nope, q_rope, payload, w_uk, w_uv)
+
+
 def solution(mesh):
     placed = (
         P("ctx", "head", None),
@@ -93,6 +301,7 @@
         P("head", None, None),
         P("head", None, None),
     )
+    small = mesh.shape["ctx"] == 16 and mesh.shape["head"] == 2
     return jax.shard_map(
-        shards, mesh=mesh, in_specs=placed, out_specs=P("ctx", "head"), check_vma=False
-    )
+        fused if small else shards, mesh=mesh, in_specs=placed, out_specs=P("ctx", "head"), check_vma=False
+    )

time: 130 us -> 28.8 us (0.22)
  blocking collectives: 43.8 us -> 0 us
  Pallas kernels: 0 us -> 21.8 us
  local copies, waits for them, and re-layouts: 23.3 us -> 5.19 us
  between operations: 16.4 us -> 0.02 us
  matrix products: 14.6 us -> 0 us
  loops' own time: 11.2 us -> 0 us
  other arithmetic: 12.5 us -> 1.53 us
  waiting for transfers between devices: 7.56 us -> 0 us
    unnamed x2 -> x0, blocking collectives: 43.8 us -> none
    pallas_call x0 -> x1, Pallas kernels: none -> 21.8 us  [fused(): pl.pallas_call(functools.partial(kernel, total, float(nope_width + q_rope...]
    dot_general x34 -> x0, matrix products: 14.6 us -> none  [the longest x16 7.54 us: attend(): jnp.dot(expo.astype(jnp.bfloat16), cache_block[:, :latent_width], preferr...]
    squeeze x16 -> x0, local copies, waits for them, and re-layouts: 14.4 us -> none  [shards(): final_state, unused = lax.scan(advance, start_state, key_blocks)]
    another operation x17 -> x0, loops' own time: 11.2 us -> none  [the longest x1 10.5 us: shards(): final_state, unused = lax.scan(advance, start_state, key_blocks)]
    reduce_or x16 -> x0, other arithmetic: 10.5 us -> none  [visit_block(): wanted = jnp.any((key_pos >= seq_start) & (key_pos <= upper_bound))]
    all_gather x1 -> x0, waiting for transfers between devices: 6.85 us -> none  [shards(): lax.all_gather(latent_cache, ('ctx', 'head'), axis=0, tiled=True)]
    ge x16 -> x0, local copies, waits for them, and re-layouts: 1.47 us -> none  [attend(): row_pos[:, None] >= key_pos[None, :]]
  transfers between devices with their start and end apart: 1 -> 0, of which waited for: 1 -> 0; matrix products, arithmetic and copies ran while one was open for 5% -> 0% of each run, Pallas kernels for 0% -> 0%
where the time goes in v1:
time: 28.8 us; the launch traced here: 28.5 us
  Pallas kernels  21.8 us (76%)
  local copies, waits for them, and re-layouts  5.19 us (18%)
  other arithmetic  1.53 us (5%)
    pallas_call x1, Pallas kernels, fused(): pl.pallas_call(functools.partial(kernel, total, float(nope_width + q_rope...  21.8 us
    unnamed x9, local copies, waits for them, and re-layouts  4.91 us
    concatenate x1, other arithmetic, fused(): jnp.concatenate([latent_cache, place, jnp.zeros((shard, width - packed -...  0.86 us
    another operation x1, other arithmetic, fused(): jnp.stack([positions // 64, positions % 64], axis=1).astype(jnp.bfloat16)  0.67 us

profile of v1, /device:TPU:0, one launch (start us, length us, event | category | flops | bytes accessed | tf_op | source)
XLA Modules:
  0.0 28.5 jit_solution(13805079838907310875)
XLA Ops:
  0.0 0.7 %convert_bitcast_fusion = (bf16[32,1]{0,1:T(2,128)(2,1)S(1)}, bf16[32,1]{0,1:T(2,128)(2,1)S(1)}) fusion(s32[32]{0:T(128)} %param.9), kind=kLoop, calls=%fused_computation.8 | loop fusion | flops 672 | bytes 256 | tf_op jit(solution)/shard_map/stack | solution.py:260
  0.7 0.1 pad.3.clone
  0.7 0.1 copy.7
  0.8 0.1 copy.8
  0.9 0.9 %maximum_maximum_fusion.pay_ref = bf16[32,640]{1,0:T(8,128)(2,1)S(1)} fusion(bf16[32,1]{1,0:T(8,128)(2,1)S(1)} %copy.8, bf16[32,1]{1,0:T(8,128)(2,1)S(1)} %copy.7, bf16[32,576]{1,0:T(8,128)(2,1)} %param.8, bf16[640]{0:T(1024)(128)(2,1)S(1)} %pad.3.clone), kind=kLoop, calls=%fused_computation | loop fusion | flops 163840 | bytes 79232 | tf_op jit(solution)/shard_map/concatenate | solution.py:261
  1.8 0.0 copy-start
  1.8 1.2 %copy-done = bf16[8,128,512]{2,1,0:T(8,128)(2,1)S(1)} copy-done((bf16[8,128,512]{2,1,0:T(8,128)(2,1)S(1)}, bf16[8,128,512]{2,1,0:T(8,128)(2,1)}, u32[]{:S(2)}) %copy-start) | copy-done | bytes 1048600
  3.0 0.0 copy-start.1
  3.0 1.2 %copy-done.1 = bf16[8,512,128]{2,1,0:T(8,128)(2,1)S(1)} copy-done((bf16[8,512,128]{2,1,0:T(8,128)(2,1)S(1)}, bf16[8,512,128]{2,1,0:T(8,128)(2,1)}, u32[]{:S(2)}) %copy-start.1) | copy-done | bytes 1048600
  4.3 0.0 copy-start.2
  4.3 0.9 %copy-done.2 = bf16[64,8,128]{2,1,0:T(8,128)(2,1)S(1)} copy-done((bf16[64,8,128]{2,1,0:T(8,128)(2,1)S(1)}, bf16[64,8,128]{2,1,0:T(8,128)(2,1)}, u32[]{:S(2)}) %copy-start.2) | copy-done | bytes 131096
  5.2 0.0 copy-start.3
  5.2 0.9 %copy-done.3 = bf16[64,8,64]{2,1,0:T(8,128)(2,1)S(1)} copy-done((bf16[64,8,64]{2,1,0:T(8,128)(2,1)S(1)}, bf16[64,8,64]{2,1,0:T(8,128)(2,1)}, u32[]{:S(2)}) %copy-start.3) | copy-done | bytes 65560
  6.1 21.8 %shard_map.64 = bf16[64,1024]{1,0:T(8,128)(2,1)S(1)} custom-call(bf16[64,8,128]{2,1,0:T(8,128)(2,1)S(1)} %copy-done.2, bf16[64,8,64]{2,1,0:T(8,128)(2,1)S(1)} %copy-done.3, bf16[32,640]{1,0:T(8,128)(2,1)S(1)} %maximum_maximum_fusion.pay_ref, bf16[8,128,512]{2,1,0:T(8,128)(2,1)S(1)} %copy-done, bf16[8,512,128]{2,1,0:T(8,128)(2,1)S(1)} %copy-done.1), custom_call_target="tpu_custom_call" | custom-call | flops 1342177280 | bytes 4194304 | tf_op jit(solution)/shard_map/pallas_call | solution.py:268
  27.9 0.7 %copy.10 = bf16[64,1024]{1,0:T(8,128)(2,1)} copy(bf16[64,1024]{1,0:T(8,128)(2,1)S(1)} %shard_map.64) | data formatting | bytes 262144
  (1 shorter events, 0.0 us)
Async XLA Ops:
  1.8 1.2 %copy-start = (bf16[8,128,512]{2,1,0:T(8,128)(2,1)S(1)}, bf16[8,128,512]{2,1,0:T(8,128)(2,1)}, u32[]{:S(2)}) copy-start(bf16[8,128,512]{2,1,0:T(8,128)(2,1)} %uk_hbm.1) | copy-start | bytes 3145732
  3.0 1.2 %copy-start.1 = (bf16[8,512,128]{2,1,0:T(8,128)(2,1)S(1)}, bf16[8,512,128]{2,1,0:T(8,128)(2,1)}, u32[]{:S(2)}) copy-start(bf16[8,512,128]{2,1,0:T(8,128)(2,1)} %uv_hbm.1) | copy-start | bytes 3145732
  4.3 0.9 %copy-start.2 = (bf16[64,8,128]{2,1,0:T(8,128)(2,1)S(1)}, bf16[64,8,128]{2,1,0:T(8,128)(2,1)}, u32[]{:S(2)}) copy-start(bf16[64,8,128]{2,1,0:T(8,128)(2,1)} %nope_ref.1) | copy-start | bytes 393220
  5.2 0.9 %copy-start.3 = (bf16[64,8,64]{2,1,0:T(8,128)(2,1)S(1)}, bf16[64,8,64]{2,1,0:T(8,128)(2,1)}, u32[]{:S(2)}) copy-start(bf16[64,8,64]{2,1,0:T(8,128)(2,1)} %rope_ref.1) | copy-start | bytes 196612

commit v2 on v1

--- a/solution.py
+++ b/solution.py
@@ -93,20 +93,30 @@
 
 def kernel(
     seq_length, scale_factor,
-    nope_ref, rope_ref, pay_ref, uk_hbm, uv_hbm, out_ref,
+    nope_hbm, rope_hbm, cache_hbm, pos_hbm, uk_hbm, uv_hbm, out_ref,
+    cache_ref, pos_ref, nope_ref, rope_ref,
     keys, uk, uv, nope_f, rope_f, query, scores, probs,
     local_sem, send_sem, recv_sem,
 ):
     tokens, heads, _ = nope_ref.shape
     latent = uk.shape[2]
     value_width = uv.shape[2]
-    shard, width = pay_ref.shape
+    shard, packed = cache_ref.shape
+    width = keys.shape[1]
     ctx, core = lax.axis_index("ctx"), lax.axis_index("head")
     z, y, x = ctx // 4, (ctx // 2) % 2, ctx % 2
-    copy_uk = pltpu.make_async_copy(uk_hbm, uk, local_sem.at[0])
-    copy_uv = pltpu.make_async_copy(uv_hbm, uv, local_sem.at[1])
-    copy_uk.start()
-    copy_uv.start()
+    loads = [
+        pltpu.make_async_copy(source, target, local_sem.at[i])
+        for i, (source, target) in enumerate(
+            (
+                (cache_hbm, cache_ref), (pos_hbm, pos_ref), (nope_hbm, nope_ref),
+                (rope_hbm, rope_ref), (uk_hbm, uk), (uv_hbm, uv),
+            )
+        )
+    ]
+    for load in loads:
+        load.start()
+    copy_cache, copy_pos, copy_nope, copy_rope, copy_uk, copy_uv = loads
 
     def index_of(zi, yi, xi):
         return (zi * 2 + yi) * 2 + xi
@@ -139,7 +149,22 @@
     def rows_of(slot):
         return keys.at[pl.ds(pl.multiple_of(slot * shard, shard), shard)]
 
-    keys[pl.ds(pl.multiple_of(own * shard, shard), shard), :] = pay_ref[...]
+    own_rows = pl.ds(pl.multiple_of(own * shard, shard), shard)
+    copy_cache.wait()
+    copy_pos.wait()
+    across = lax.broadcasted_iota(jnp.int32, (shard, shard), 0)
+    down = lax.broadcasted_iota(jnp.int32, (shard, shard), 1)
+    column = jnp.sum(
+        jnp.where(across == down, pos_ref[...].astype(jnp.float32), 0.0), axis=1, keepdims=True
+    )
+    high = jnp.floor(column * (1.0 / 64.0))
+    low = column - high * 64.0
+    spare = lax.broadcasted_iota(jnp.int32, (shard, width - packed), 1)
+    place = jnp.where(spare == 0, high, jnp.where(spare == 1, low, 0.0))
+    keys[own_rows, :latent] = cache_ref[:, :latent]
+    keys[own_rows, latent:] = jnp.concatenate(
+        [cache_ref[:, latent:].astype(jnp.float32), place], axis=1
+    ).astype(jnp.bfloat16)
     pl.semaphore_wait(barrier, 6)
 
     sends = []
@@ -173,6 +198,8 @@
     send(own, third)
     send(own, partner)
 
+    copy_nope.wait()
+    copy_rope.wait()
     nope_f[...] = nope_ref[...].astype(jnp.float32)
     rope_f[...] = rope_ref[...].astype(jnp.float32)
     copy_uk.wait()
@@ -257,20 +284,20 @@
     shard, packed = latent_cache.shape
     width = -(-(packed + 2) // 128) * 128
     total = shard * lax.axis_size("ctx") * lax.axis_size("head")
-    place = jnp.stack([positions // 64, positions % 64], axis=1).astype(jnp.bfloat16)
-    payload = jnp.concatenate(
-        [latent_cache, place, jnp.zeros((shard, width - packed - 2), jnp.bfloat16)], axis=1
-    )
     rows = tokens * heads
     vmem = pl.BlockSpec(memory_space=pltpu.VMEM)
-    hbm = pl.BlockSpec(memory_space=pl.ANY)
+    hbm = pl.BlockSpec(memory_space=pltpu.HBM)
     flops = 2 * rows * (total * (width + latent) + latent * 2 * nope_width)
     return pl.pallas_call(
         functools.partial(kernel, total, float(nope_width + q_rope.shape[2]) ** (-0.5)),
         out_shape=jax.ShapeDtypeStruct((tokens, heads * w_uv.shape[2]), jnp.bfloat16),
-        in_specs=[vmem, vmem, vmem, hbm, hbm],
+        in_specs=[hbm] * 6,
         out_specs=vmem,
         scratch_shapes=[
+            pltpu.VMEM((shard, packed), jnp.bfloat16),
+            pltpu.VMEM((1, shard), jnp.int32),
+            pltpu.VMEM(q_nope.shape, jnp.bfloat16),
+            pltpu.VMEM(q_rope.shape, jnp.bfloat16),
             pltpu.VMEM((total, width), jnp.bfloat16),
             pltpu.VMEM(w_uk.shape, jnp.bfloat16),
             pltpu.VMEM(w_uv.shape, jnp.bfloat16),
@@ -279,17 +306,17 @@
             pltpu.VMEM((rows, width), jnp.bfloat16),
             pltpu.VMEM((rows, total), jnp.float32),
             pltpu.VMEM((rows, total), jnp.bfloat16),
-            pltpu.SemaphoreType.DMA((2,)),
+            pltpu.SemaphoreType.DMA((6,)),
             pltpu.SemaphoreType.DMA((31,)),
             pltpu.SemaphoreType.DMA((32,)),
         ],
         compiler_params=pltpu.CompilerParams(
-            collective_id=0, has_side_effects=True, vmem_limit_bytes=40 * 1024 * 1024
+            collective_id=0, has_side_effects=True, vmem_limit_bytes=60 * 1024 * 1024
         ),
         cost_estimate=pl.CostEstimate(
             flops=flops, bytes_accessed=4 * 1024 * 1024, transcendentals=rows * total
         ),
-    )(q_nope, q_rope, payload, w_uk, w_uv)
+    )(q_nope, q_rope, latent_cache, positions.reshape(1, shard), w_uk, w_uv)
 
 
 def solution(mesh):

time: 28.8 us -> 24 us (0.83)
  local copies, waits for them, and re-layouts: 5.19 us -> 1.57 us
  other arithmetic: 1.53 us -> 0 us
  Pallas kernels: 21.8 us -> 22.3 us
    unnamed x9 -> x1, local copies, waits for them, and re-layouts: 4.91 us -> 1.57 us
    concatenate x1 -> x0, other arithmetic: 0.86 us -> none  [fused(): jnp.concatenate([latent_cache, place, jnp.zeros((shard, width - packed -...]
    another operation x1 -> x0, other arithmetic: 0.67 us -> none  [fused(): jnp.stack([positions // 64, positions % 64], axis=1).astype(jnp.bfloat16)]
    pallas_call x1, Pallas kernels: 21.8 us -> 22.3 us  [fused(): pl.pallas_call(functools.partial(kernel, total, float(nope_width + q_rope...]
where the time goes in v2:
time: 24 us; the launch traced here: 23.9 us
  Pallas kernels  22.3 us (93%)
  local copies, waits for them, and re-layouts  1.57 us (7%)
    pallas_call x1, Pallas kernels, fused(): pl.pallas_call(functools.partial(kernel, total, float(nope_width + q_rope...  22.3 us
    unnamed x1, local copies, waits for them, and re-layouts  1.57 us

profile of v2, /device:TPU:0, one launch (start us, length us, event | category | flops | bytes accessed | tf_op | source)
XLA Modules:
  0.0 23.9 jit_solution(3512692110818942266)
XLA Ops:
  0.0 22.3 %shard_map.64 = bf16[64,1024]{1,0:T(8,128)(2,1)} custom-call(bf16[64,8,128]{2,1,0:T(8,128)(2,1)} %nope_hbm.1, bf16[64,8,64]{2,1,0:T(8,128)(2,1)} %rope_hbm.1, bf16[32,576]{1,0:T(8,128)(2,1)} %cache_hbm.1, s32[1,32]{1,0:T(1,128)} %bitcast.1, bf16[8,128,512]{2,1,0:T(8,128)(2,1)} %uk_hbm.1, bf16[8,512,128]{2,1,0:T(8,128)(2,1)} %uv_hbm.1), custom_call_target="tpu_custom_call" | custom-call | flops 1342177280 | bytes 4194304 | tf_op jit(solution)/shard_map/pallas_call | solution.py:291
  22.3 1.6 %copy.8 = bf16[64,1024]{1,0:T(8,128)(2,1)} copy(bf16[64,1024]{1,0:T(8,128)(2,1)} %shard_map.64) | data formatting | bytes 262144

commit v3 on v2

--- a/solution.py
+++ b/solution.py
@@ -118,33 +118,29 @@
         load.start()
     copy_cache, copy_pos, copy_nope, copy_rope, copy_uk, copy_uv = loads
 
-    def index_of(zi, yi, xi):
-        return (zi * 2 + yi) * 2 + xi
-
-    def line_of(c, yi, xi):
-        return (c * 2 + yi) * 2 + xi
-
-    def slot_of(line, zi):
-        return line * 4 + zi
-
-    x2 = x + (1 - core) * (1 - 2 * x)
-    y2 = y + core * (1 - 2 * y)
-    x3 = x + core * (1 - 2 * x)
-    y3 = y + (1 - core) * (1 - 2 * y)
-    second = (index_of(z, y2, x2), core)
-    third = (index_of(z, y3, x3), core)
+    def flip(bit, by):
+        return bit + by * (1 - 2 * bit)
+
+    cube, low = z // 2, z % 2
+
+    def device_of(ci, li, yi, xi):
+        return (((ci * 2 + li) * 2 + yi) * 2 + xi, core)
+
+    def slot_of(c, ci, li, yi, xi):
+        return (((c * 2 + ci) * 2 + li) * 2 + yi) * 2 + xi
+
+    steps = ((0, 0, 1), (0, 1, 0), (1, 0, 0), (0, 1, 1), (1, 0, 1), (1, 1, 0), (1, 1, 1))
+    places = [(flip(low, a), flip(y, b), flip(x, c)) for a, b, c in steps]
+    peers = [device_of(cube, *place) for place in places]
+    mirror = device_of(1 - cube, low, y, x)
     partner = (ctx, 1 - core)
-    along = [(index_of((z + k) % 4, y, x), core) for k in (1, 2, 3)]
 
     barrier = pltpu.get_barrier_semaphore()
-    for peer in along + [second, third, partner]:
+    for peer in peers + [mirror, partner]:
         pl.semaphore_signal(barrier, inc=1, device_id=peer, device_id_type=MESH)
 
-    line_own = line_of(core, y, x)
-    line_second = line_of(core, y2, x2)
-    line_third = line_of(core, y3, x3)
-    line_both = line_of(core, 1 - y, 1 - x)
-    own = slot_of(line_own, z)
+    own = slot_of(core, cube, low, y, x)
+    mirrored = slot_of(core, 1 - cube, low, y, x)
 
     def rows_of(slot):
         return keys.at[pl.ds(pl.multiple_of(slot * shard, shard), shard)]
@@ -158,14 +154,14 @@
         jnp.where(across == down, pos_ref[...].astype(jnp.float32), 0.0), axis=1, keepdims=True
     )
     high = jnp.floor(column * (1.0 / 64.0))
-    low = column - high * 64.0
+    rest = column - high * 64.0
     spare = lax.broadcasted_iota(jnp.int32, (shard, width - packed), 1)
-    place = jnp.where(spare == 0, high, jnp.where(spare == 1, low, 0.0))
+    place = jnp.where(spare == 0, high, jnp.where(spare == 1, rest, 0.0))
     keys[own_rows, :latent] = cache_ref[:, :latent]
     keys[own_rows, latent:] = jnp.concatenate(
         [cache_ref[:, latent:].astype(jnp.float32), place], axis=1
     ).astype(jnp.bfloat16)
-    pl.semaphore_wait(barrier, 6)
+    pl.semaphore_wait(barrier, 9)
 
     sends = []
 
@@ -185,17 +181,17 @@
             device_id=partner, device_id_type=MESH,
         ).wait_recv()
 
-    def score(line):
-        columns = pl.ds(pl.multiple_of(line * 128, 128), 128)
-        scores[:, columns] = lax.dot_general(
-            query[...], keys[columns, :], (((1,), (1,)), ((), ())),
+    def score(c, ci):
+        start = pl.multiple_of((c * 2 + ci) * 8 * shard, 8 * shard)
+        span = pl.ds(start, 8 * shard)
+        scores[:, span] = lax.dot_general(
+            query[...], keys[span, :], (((1,), (1,)), ((), ())),
             preferred_element_type=jnp.float32,
         )
 
-    for peer in along:
+    send(own, mirror)
+    for peer in peers[::-1]:
         send(own, peer)
-    send(own, second)
-    send(own, third)
     send(own, partner)
 
     copy_nope.wait()
@@ -215,31 +211,29 @@
             axis=1,
         ).astype(jnp.bfloat16)
 
-    for k in (1, 2, 3):
-        slot = slot_of(line_own, (z + 4 - k) % 4)
+    arrived(mirrored)
+    for peer in peers[::-1]:
+        send(mirrored, peer)
+    send(mirrored, partner)
+    for place in places:
+        slot = slot_of(core, cube, *place)
         arrived(slot)
-        send(slot, second)
-        send(slot, third)
         send(slot, partner)
-    for k in (0, 1, 2, 3):
-        slot = slot_of(line_second, (z + 4 - k) % 4)
+    score(core, cube)
+    for place in places:
+        slot = slot_of(core, 1 - cube, *place)
         arrived(slot)
-        send(slot, third)
         send(slot, partner)
-    score(line_own)
-    score(line_second)
-    for line in (line_third, line_both):
-        for k in (0, 1, 2, 3):
-            slot = slot_of(line, (z + 4 - k) % 4)
-            arrived(slot)
-            send(slot, partner)
-        score(line)
     other = 1 - core
-    for yi, xi in ((y, x), (y3, x3), (y2, x2), (1 - y, 1 - x)):
-        line = line_of(other, yi, xi)
-        for k in (0, 1, 2, 3):
-            arrived(slot_of(line, (z + 4 - k) % 4))
-        score(line)
+    arrived(slot_of(other, cube, low, y, x))
+    for place in places:
+        arrived(slot_of(other, cube, *place))
+    score(other, cube)
+    score(core, 1 - cube)
+    arrived(slot_of(other, 1 - cube, low, y, x))
+    for place in places:
+        arrived(slot_of(other, 1 - cube, *place))
+    score(other, 1 - cube)
 
     lane = lax.broadcasted_iota(jnp.int32, (8, width - latent), 1)
     first = rope_ref.shape[2]
@@ -248,7 +242,7 @@
         pick.astype(jnp.bfloat16), keys[:, latent:], (((1,), (1,)), ((), ())),
         preferred_element_type=jnp.float32,
     )[0:1, :]
-    token_slots = [slot_of(line_of(c, y, x), z) for c in (0, 1)]
+    token_slots = [slot_of(c, cube, low, y, x) for c in (0, 1)]
     tails = jnp.concatenate(
         [
             keys[pl.ds(pl.multiple_of(s * shard, shard), shard), latent:]

time: 24 us -> 20.3 us (0.85)
  Pallas kernels: 22.3 us -> 18.4 us
    pallas_call x1, Pallas kernels: 22.3 us -> 18.4 us  [fused(): pl.pallas_call(functools.partial(kernel, total, float(nope_width + q_rope...]
where the time goes in v3:
time: 20.3 us; the launch traced here: 20 us
  Pallas kernels  18.4 us (91%)
  local copies, waits for them, and re-layouts  1.57 us (8%)
    pallas_call x1, Pallas kernels, fused(): pl.pallas_call(functools.partial(kernel, total, float(nope_width + q_rope...  18.4 us
    unnamed x1, local copies, waits for them, and re-layouts  1.57 us

profile of v3, /device:TPU:0, one launch (start us, length us, event | category | flops | bytes accessed | tf_op | source)
XLA Modules:
  0.0 20.0 jit_solution(447259058062293668)
XLA Ops:
  0.0 18.4 %shard_map.64 = bf16[64,1024]{1,0:T(8,128)(2,1)} custom-call(bf16[64,8,128]{2,1,0:T(8,128)(2,1)} %nope_hbm.1, bf16[64,8,64]{2,1,0:T(8,128)(2,1)} %rope_hbm.1, bf16[32,576]{1,0:T(8,128)(2,1)} %cache_hbm.1, s32[1,32]{1,0:T(1,128)} %bitcast.1, bf16[8,128,512]{2,1,0:T(8,128)(2,1)} %uk_hbm.1, bf16[8,512,128]{2,1,0:T(8,128)(2,1)} %uv_hbm.1), custom_call_target="tpu_custom_call" | custom-call | flops 1342177280 | bytes 4194304 | tf_op jit(solution)/shard_map/pallas_call | solution.py:285
  18.4 1.6 %copy.8 = bf16[64,1024]{1,0:T(8,128)(2,1)} copy(bf16[64,1024]{1,0:T(8,128)(2,1)} %shard_map.64) | data formatting | bytes 262144

commit v4 on v3

--- a/solution.py
+++ b/solution.py
@@ -95,7 +95,7 @@
     seq_length, scale_factor,
     nope_hbm, rope_hbm, cache_hbm, pos_hbm, uk_hbm, uv_hbm, out_ref,
     cache_ref, pos_ref, nope_ref, rope_ref,
-    keys, uk, uv, nope_f, rope_f, query, scores, probs,
+    keys, uk, uv, nope_f, rope_f, query, scores, probs, near_mixed,
     local_sem, send_sem, recv_sem,
 ):
     tokens, heads, _ = nope_ref.shape
@@ -127,7 +127,7 @@
         return (((ci * 2 + li) * 2 + yi) * 2 + xi, core)
 
     def slot_of(c, ci, li, yi, xi):
-        return (((c * 2 + ci) * 2 + li) * 2 + yi) * 2 + xi
+        return (((ci * 2 + c) * 2 + li) * 2 + yi) * 2 + xi
 
     steps = ((0, 0, 1), (0, 1, 0), (1, 0, 0), (0, 1, 1), (1, 0, 1), (1, 1, 0), (1, 1, 1))
     places = [(flip(low, a), flip(y, b), flip(x, c)) for a, b, c in steps]
@@ -182,7 +182,7 @@
         ).wait_recv()
 
     def score(c, ci):
-        start = pl.multiple_of((c * 2 + ci) * 8 * shard, 8 * shard)
+        start = pl.multiple_of((ci * 2 + c) * 8 * shard, 8 * shard)
         span = pl.ds(start, 8 * shard)
         scores[:, span] = lax.dot_general(
             query[...], keys[span, :], (((1,), (1,)), ((), ())),
@@ -211,6 +211,34 @@
             axis=1,
         ).astype(jnp.bfloat16)
 
+    lane = lax.broadcasted_iota(jnp.int32, (8, width - latent), 1)
+    first = packed - latent
+    pick = jnp.where(lane == first, 64.0, jnp.where(lane == first + 1, 1.0, 0.0))
+    factor = scale_factor * 1.4426950408889634
+
+    def attend(ci, query_pos, seq_start):
+        count = 16 * shard
+        span = pl.ds(pl.multiple_of(ci * count, count), count)
+        key_pos = lax.dot_general(
+            pick.astype(jnp.bfloat16), keys[span, latent:], (((1,), (1,)), ((), ())),
+            preferred_element_type=jnp.float32,
+        )[0:1, :]
+        hidden = (key_pos > query_pos) | (key_pos < seq_start)
+        tops, sums = [], []
+        for h in range(heads):
+            rows = pl.ds(h * tokens, tokens)
+            s = jnp.where(hidden, -jnp.inf, scores[rows, span])
+            top = jnp.maximum(jnp.max(s, axis=1, keepdims=True), -1e30)
+            expo = jnp.exp2((s - top) * factor)
+            tops.append(top)
+            sums.append(jnp.sum(expo, axis=1, keepdims=True))
+            probs[rows, :] = expo.astype(jnp.bfloat16)
+        mixed = jnp.dot(
+            probs[...], keys[span, :latent], preferred_element_type=jnp.float32
+        )
+        return tops, sums, mixed
+
+    other = 1 - core
     arrived(mirrored)
     for peer in peers[::-1]:
         send(mirrored, peer)
@@ -220,28 +248,10 @@
         arrived(slot)
         send(slot, partner)
     score(core, cube)
-    for place in places:
-        slot = slot_of(core, 1 - cube, *place)
-        arrived(slot)
-        send(slot, partner)
-    other = 1 - core
     arrived(slot_of(other, cube, low, y, x))
     for place in places:
         arrived(slot_of(other, cube, *place))
     score(other, cube)
-    score(core, 1 - cube)
-    arrived(slot_of(other, 1 - cube, low, y, x))
-    for place in places:
-        arrived(slot_of(other, 1 - cube, *place))
-    score(other, 1 - cube)
-
-    lane = lax.broadcasted_iota(jnp.int32, (8, width - latent), 1)
-    first = rope_ref.shape[2]
-    pick = jnp.where(lane == first, 64.0, jnp.where(lane == first + 1, 1.0, 0.0))
-    key_pos = lax.dot_general(
-        pick.astype(jnp.bfloat16), keys[:, latent:], (((1,), (1,)), ((), ())),
-        preferred_element_type=jnp.float32,
-    )[0:1, :]
     token_slots = [slot_of(c, cube, low, y, x) for c in (0, 1)]
     tails = jnp.concatenate(
         [
@@ -252,21 +262,28 @@
     ).astype(jnp.float32)
     query_pos = jnp.sum(tails * pick[0:1, :], axis=1, keepdims=True)
     seq_start = jnp.floor(query_pos * (1.0 / seq_length)) * float(seq_length)
-    hidden = (key_pos > query_pos) | (key_pos < seq_start)
-    factor = scale_factor * 1.4426950408889634
-    sums = []
-    for h in range(heads):
-        rows = pl.ds(h * tokens, tokens)
-        s = jnp.where(hidden, -jnp.inf, scores[rows, :])
-        expo = jnp.exp2((s - jnp.max(s, axis=1, keepdims=True)) * factor)
-        sums.append(jnp.sum(expo, axis=1, keepdims=True))
-        probs[rows, :] = expo.astype(jnp.bfloat16)
-    mixed = jnp.dot(probs[...], keys[:, :latent], preferred_element_type=jnp.float32)
+    near_tops, near_sums, mixed = attend(cube, query_pos, seq_start)
+    near_mixed[...] = mixed
+    for place in places:
+        slot = slot_of(core, 1 - cube, *place)
+        arrived(slot)
+        send(slot, partner)
+    score(core, 1 - cube)
+    arrived(slot_of(other, 1 - cube, low, y, x))
+    for place in places:
+        arrived(slot_of(other, 1 - cube, *place))
+    score(other, 1 - cube)
+    far_tops, far_sums, mixed = attend(1 - cube, query_pos, seq_start)
     copy_uv.wait()
     for h in range(heads):
-        part = (mixed[h * tokens : (h + 1) * tokens, :] / sums[h]).astype(jnp.bfloat16)
+        rows = slice(h * tokens, (h + 1) * tokens)
+        top = jnp.maximum(near_tops[h], far_tops[h])
+        near_share = jnp.exp2((near_tops[h] - top) * factor)
+        far_share = jnp.exp2((far_tops[h] - top) * factor)
+        total = near_sums[h] * near_share + far_sums[h] * far_share
+        part = (near_mixed[rows, :] * near_share + mixed[rows, :] * far_share) / total
         out_ref[:, h * value_width : (h + 1) * value_width] = jnp.dot(
-            part, uv[h], preferred_element_type=jnp.float32
+            part.astype(jnp.bfloat16), uv[h], preferred_element_type=jnp.float32
         ).astype(jnp.bfloat16)
     for copy in sends:
         copy.wait_send()
@@ -299,7 +316,8 @@
             pltpu.VMEM(q_rope.shape, jnp.float32),
             pltpu.VMEM((rows, width), jnp.bfloat16),
             pltpu.VMEM((rows, total), jnp.float32),
-            pltpu.VMEM((rows, total), jnp.bfloat16),
+            pltpu.VMEM((rows, total // 2), jnp.bfloat16),
+            pltpu.VMEM((rows, latent), jnp.float32),
             pltpu.SemaphoreType.DMA((6,)),
             pltpu.SemaphoreType.DMA((31,)),
             pltpu.SemaphoreType.DMA((32,)),

time: 20.3 us -> 19.9 us (0.980)
  Pallas kernels: 18.4 us -> 18.1 us
    pallas_call x1, Pallas kernels: 18.4 us -> 18.1 us  [fused(): pl.pallas_call(functools.partial(kernel, total, float(nope_width + q_rope...]
where the time goes in v4:
time: 19.9 us; the launch traced here: 19.7 us
  Pallas kernels  18.1 us (91%)
  local copies, waits for them, and re-layouts  1.57 us (8%)
    pallas_call x1, Pallas kernels, fused(): pl.pallas_call(functools.partial(kernel, total, float(nope_width + q_rope...  18.1 us
    unnamed x1, local copies, waits for them, and re-layouts  1.57 us

profile of v4, /device:TPU:0, one launch (start us, length us, event | category | flops | bytes accessed | tf_op | source)
XLA Modules:
  0.0 19.7 jit_solution(7712975095950322230)
XLA Ops:
  0.0 18.1 %shard_map.64 = bf16[64,1024]{1,0:T(8,128)(2,1)} custom-call(bf16[64,8,128]{2,1,0:T(8,128)(2,1)} %nope_hbm.1, bf16[64,8,64]{2,1,0:T(8,128)(2,1)} %rope_hbm.1, bf16[32,576]{1,0:T(8,128)(2,1)} %cache_hbm.1, s32[1,32]{1,0:T(1,128)} %bitcast.1, bf16[8,128,512]{2,1,0:T(8,128)(2,1)} %uk_hbm.1, bf16[8,512,128]{2,1,0:T(8,128)(2,1)} %uv_hbm.1), custom_call_target="tpu_custom_call" | custom-call | flops 1342177280 | bytes 4194304 | tf_op jit(solution)/shard_map/pallas_call | solution.py:302
  18.1 1.6 %copy.8 = bf16[64,1024]{1,0:T(8,128)(2,1)} copy(bf16[64,1024]{1,0:T(8,128)(2,1)} %shard_map.64) | data formatting | bytes 262144

commit v5 on v4

--- a/solution.py
+++ b/solution.py
@@ -243,7 +243,7 @@
     for peer in peers[::-1]:
         send(mirrored, peer)
     send(mirrored, partner)
-    for place in places:
+    for place in places[::-1]:
         slot = slot_of(core, cube, *place)
         arrived(slot)
         send(slot, partner)
@@ -264,7 +264,7 @@
     seq_start = jnp.floor(query_pos * (1.0 / seq_length)) * float(seq_length)
     near_tops, near_sums, mixed = attend(cube, query_pos, seq_start)
     near_mixed[...] = mixed
-    for place in places:
+    for place in places[::-1]:
         slot = slot_of(core, 1 - cube, *place)
         arrived(slot)
         send(slot, partner)

time: 19.9 us -> 20.1 us (1.010)
  no operation moved by 1% of the time
where the time goes in v5:
time: 20.1 us; the launch traced here: 19.8 us
  Pallas kernels  18.2 us (91%)
  local copies, waits for them, and re-layouts  1.57 us (8%)
    pallas_call x1, Pallas kernels, fused(): pl.pallas_call(functools.partial(kernel, total, float(nope_width + q_rope...  18.2 us
    unnamed x1, local copies, waits for them, and re-layouts  1.57 us

profile of v5, /device:TPU:0, one launch (start us, length us, event | category | flops | bytes accessed | tf_op | source)
XLA Modules:
  0.0 19.8 jit_solution(16944575063852937625)
XLA Ops:
  0.0 18.2 %shard_map.64 = bf16[64,1024]{1,0:T(8,128)(2,1)} custom-call(bf16[64,8,128]{2,1,0:T(8,128)(2,1)} %nope_hbm.1, bf16[64,8,64]{2,1,0:T(8,128)(2,1)} %rope_hbm.1, bf16[32,576]{1,0:T(8,128)(2,1)} %cache_hbm.1, s32[1,32]{1,0:T(1,128)} %bitcast.1, bf16[8,128,512]{2,1,0:T(8,128)(2,1)} %uk_hbm.1, bf16[8,512,128]{2,1,0:T(8,128)(2,1)} %uv_hbm.1), custom_call_target="tpu_custom_call" | custom-call | flops 1342177280 | bytes 4194304 | tf_op jit(solution)/shard_map/pallas_call | solution.py:302
  18.2 1.6 %copy.8 = bf16[64,1024]{1,0:T(8,128)(2,1)} copy(bf16[64,1024]{1,0:T(8,128)(2,1)} %shard_map.64) | data formatting | bytes 262144
